TPU v7x, 128 devices: a whole 4x4x4 slice. The times are simulated.
128 devices in a mesh: row: 8 (over z, core), col: 16 (over y, x).
Axes of the slice: x: 4, y: 4, z: 4, core: 2. Of those that a mesh axis runs over, the one named last changes fastest.
Arguments:
- working: float32 [8, 8, 256, 4, 16, 256], P(None, 'row', None, None, 'col'), may hold values from -6 to 6
- factor_panel: float32 [2, 8, 8, 256, 256], P(None, None, 'row'), may hold values from -0.12 to 2, as said below
Outputs:
- gram_part: float32 [8, 8, 256, 4, 16, 256], P(None, 'row', None, None, 'col')
- finished_columns: float32 [4, 8, 256, 16, 8, 128], P(None, None, None, 'col', 'row')
Inputs may be any that keep to these rules, and one draw needn't show every extreme that they name: factor_panel holds a lower-triangular factor: entries above the factor's diagonal are zero and its diagonal entries lie between 1 and 2.
All inputs are finite; a program needn't handle non-finite values.
Results may differ from a plain program's by a relative error of at most 0.0001.
Values sent between devices are 32-bit elements; how exact they have to be, the bound alone decides.
A program may use at most 192 MiB of HBM per device.

v0:
```python
import jax
import jax.numpy as jnp
from jax import lax
from jax.sharding import PartitionSpec as P

BLK = 256
K = 30
STEPS = 2


def picked(value, axis, root):
    return lax.dynamic_index_in_dim(lax.all_gather(value, axis), root, 0, keepdims=False)


def per_device(working, factor_panel):
    row_count = lax.axis_size("row")
    col_count = lax.axis_size("col")
    row_index = lax.axis_index("row")
    blocks_rows = working.shape[0]
    width = working.shape[2]
    blocks_cols = working.shape[3]
    matrix_rows = working.reshape(blocks_rows, width, blocks_cols * width)
    global_block = jnp.arange(blocks_rows) * row_count + row_index

    def solve_row(slab, step_index):
        target = K + step_index
        owner = target % row_count
        diagonal = jnp.tril(factor_panel[step_index, target // row_count, 0])
        diagonal = jnp.where(row_index == owner, diagonal, jnp.eye(width, dtype=jnp.float32))
        solved = lax.linalg.triangular_solve(diagonal, slab, left_side=True, lower=True)
        return picked(solved, "row", owner)

    def eliminate(rows_part, blocks_part, column_part, solved, step_index):
        target = K + step_index
        updated = rows_part - jnp.einsum(
            "rab,bc->rac", column_part, solved, precision=lax.Precision.HIGHEST
        )
        below = (blocks_part > target)[:, None, None]
        here = (blocks_part == target)[:, None, None]
        return jnp.where(below, updated, jnp.where(here, solved[None], rows_part))

    solved_list = []
    solved = solve_row(matrix_rows[K // row_count], 0)
    for step_index in range(STEPS):
        solved_list.append(solved)
        if step_index + 1 < STEPS:
            slot = (K + step_index + 1) // row_count
            next_slab = eliminate(
                matrix_rows[slot : slot + 1],
                global_block[slot : slot + 1],
                factor_panel[step_index, slot : slot + 1, 0],
                solved,
                step_index,
            )
            following = solve_row(next_slab[0], step_index + 1)
        matrix_rows = eliminate(
            matrix_rows, global_block, factor_panel[step_index, :, 0], solved, step_index
        )
        if step_index + 1 < STEPS:
            solved = following
    stacked = jnp.concatenate(solved_list, 0)
    depth = stacked.shape[0]
    owners_count = col_count // row_count
    gathered = lax.all_gather(
        stacked.reshape(depth, blocks_cols, 1, width), "col", axis=2, tiled=True
    )
    gathered = gathered.reshape(depth, blocks_cols, owners_count, row_count, width)
    chosen = lax.dynamic_index_in_dim(gathered, row_index, 3, keepdims=False)
    row_panels = chosen.reshape(depth, blocks_rows * width)
    gram = lax.dot_general(
        row_panels, stacked, (((0,), (0,)), ((), ())), precision=lax.Precision.HIGHEST
    )
    gram = (gram * (1.0 / (STEPS * BLK))).reshape(blocks_rows, 1, width, blocks_cols, 1, width)
    finished_count = (K + STEPS) // row_count
    finished = matrix_rows[:finished_count].reshape(finished_count, 1, width, 1, row_count, -1)
    moved = lax.all_to_all(finished, "row", split_axis=4, concat_axis=1, tiled=True)
    return (gram, moved)


def solution(mesh):
    placed = (P(None, "row", None, None, "col", None), P(None, None, "row", None, None))
    return jax.shard_map(
        per_device,
        mesh=mesh,
        in_specs=placed,
        out_specs=(
            P(None, "row", None, None, "col", None),
            P(None, None, None, "col", "row", None),
        ),
        check_vma=False,
    )
```

profile of v0, /device:TPU:1, one launch (start us, length us, event | category | flops | bytes accessed | tf_op | source)
XLA Modules:
  0.0 434.1 jit_solution(2634957382837194387)
XLA Ops:
  8.4 3.8 while.4
  12.2 19.7 %custom-call.4 = f32[2,128,128]{1,2,0:T(8,128)S(1)} custom-call(f32[2,128,128]{2,1,0:T(8,128)S(1)} %get-tuple-element.17), custom_call_target="InvertDiagBlocksLowerTriangular" | custom-call | tf_op jit(solution)/shard_map/triangular_solve/custom-call.1 | solution.py:30
  31.9 4.2 slice_reduce_fusion
  42.2 4.1 while.5
  42.9 1.3 bitcast_dynamic-update-slice_fusion.5
  46.3 19.7 %custom-call.5 = f32[2,128,128]{1,2,0:T(8,128)S(1)} custom-call(f32[2,128,128]{2,1,0:T(8,128)S(1)} %get-tuple-element.18), custom_call_target="InvertDiagBlocksLowerTriangular" | custom-call | tf_op jit(solution)/shard_map/triangular_solve/custom-call.1 | solution.py:30
  66.0 27.0 %all-gather.8.cloned.1.call-done = f32[2048,1024]{1,0:T(8,128)} async-done(((f32[256,1024]{1,0:T(8,128)}), f32[2048,1024]{1,0:T(8,128)}) %all-gather.8.cloned.1.call-update) | async-done | bytes 8388624 | tf_op jit(solution)/shard_map/all_gather | solution.py:12
  93.0 2.9 fusion.8
  101.9 47.1 %all-gather.10.cloned.1.call-done = f32[2048,1024]{1,0:T(8,128)} async-done(((f32[256,1024]{1,0:T(8,128)}), f32[2048,1024]{1,0:T(8,128)}) %all-gather.10.cloned.1.call-update) | async-done | bytes 8388624 | tf_op jit(solution)/shard_map/all_gather | solution.py:12
  151.1 2.8 pad_maximum_fusion
  153.9 20.9 %copy.42 = f32[8,1,256,4,1,256]{2,5,3,0,4,1:T(8,128)} copy(f32[8,1,256,4,1,256]{5,4,3,2,1,0:T(1,128)} %param.4) | data formatting | bytes 16777216 | tf_op args[0]
  175.1 17.2 %convolution_bitcast_fusion.1 = f32[8,256,1024]{1,2,0:T(8,128)} fusion(f32[2,8,1,256,256]{4,3,1,2,0:T(8,128)} %bitcast.110, f32[2048,1024]{1,0:T(8,128)} %all-gather.8.cloned.1.call-done), kind=kOutput, calls=%fused_computation.11 | convolution fusion | flops 6442450944 | bytes 11534336 | tf_op jit(solution)/shard_map/rab,bc->rac/dot_general | solution.py:35
  193.6 16.5 %convolution_bitcast_fusion = f32[8,256,1024]{1,2,0:T(8,128)S(1)} fusion(f32[2,8,1,256,256]{4,3,1,2,0:T(8,128)} %bitcast.111, f32[2048,1024]{1,0:T(8,128)} %all-gather.10.cloned.1.call-done), kind=kOutput, calls=%fused_computation.10 | convolution fusion | flops 6442450944 | bytes 11534336 | tf_op jit(solution)/shard_map/rab,bc->rac/dot_general | solution.py:35
  210.2 4.9 %fusion = f32[4,256,1024]{1,2,0:T(8,128)} fusion(f32[8,256,1024]{1,2,0:T(8,128)S(1)} %convolution_bitcast_fusion, f32[8,256,1024]{1,2,0:T(8,128)S(1)} %copy-done, f32[8,256,1024]{1,2,0:T(8,128)} %bitcast.108, f32[256,1024]{0,1:T(8,128)S(1)} %copy-done.1, f32[256,1024]{0,1:T(8,128)S(1)} %copy.45, pred[4]{0:T(512)(128)(4,1)S(1)} %bitcast.117, ...), kind=kLoop, calls=%fused_computation.7 | loop fusion | flops 6291456 | bytes 18874384 | tf_op jit(solution)/shard_map/jit(_where)/select_n | solution.py:40
  215.1 5.7 %copy.49 = f32[4,1,256,1,8,128]{5,2,0,3,1,4:T(8,128)} copy(f32[4,1,256,1,8,128]{2,5,4,0,3,1:T(8,128)} %bitcast.109) | data formatting | bytes 8388608 | tf_op jit(solution)/shard_map/reshape | solution.py:75
  220.9 4.7 %all-to-all-start = ((f32[4,1,256,1,8,128]{5,2,0,3,1,4:T(8,128)}), f32[4,1,256,1,8,128]{5,2,0,3,1,4:T(8,128)}, u32[]{:S(2)}, u32[]{:S(2)}) async-start(f32[4,1,256,1,8,128]{5,2,0,3,1,4:T(8,128)} %copy.49), calls=%async_computation | async-start | bytes 8388608 | tf_op jit(solution)/shard_map/all_to_all | solution.py:76
  225.5 48.9 %all-to-all-done = f32[4,1,256,1,8,128]{5,2,0,3,1,4:T(8,128)} async-done(((f32[4,1,256,1,8,128]{5,2,0,3,1,4:T(8,128)}), f32[4,1,256,1,8,128]{5,2,0,3,1,4:T(8,128)}, u32[]{:S(2)}, u32[]{:S(2)}) %all-to-all-start) | async-done | bytes 4194336 | tf_op jit(solution)/shard_map/all_to_all | solution.py:76
  274.5 11.4 %copy.51 = f32[4,8,256,1,1,128]{5,4,3,2,1,0:T(1,128)} copy(f32[4,8,256,1,1,128]{5,2,0,1,4,3:T(8,128)} %bitcast.26) | data formatting | bytes 8388608
  285.8 64.7 %all-gather.6.cloned.1.call-done = f32[512,4,16,256]{3,0,1,2:T(8,128)} async-done(((f32[512,4,1,256]{3,0,1,2:T(8,128)}), f32[512,4,16,256]{3,0,1,2:T(8,128)}) %all-gather.6.cloned.1.call-update) | async-done | bytes 33554448 | tf_op jit(solution)/shard_map/all_gather | solution.py:64
  350.6 28.3 %copy.59 = f32[512,4,16,256]{3,2,1,0:T(8,128)S(1)} copy(f32[512,4,16,256]{3,0,1,2:T(8,128)} %all-gather.6.cloned.1.call-done) | data formatting | bytes 67108864 | tf_op jit(solution)/shard_map/all_gather | solution.py:64
  378.8 6.6 %constant_dynamic-slice_fusion.2 = f32[512,4,2,1,256]{4,3,2,1,0:T(1,128)} fusion(f32[512,4,2,8,256]{4,3,2,1,0:T(8,128)S(1)} %bitcast.106, s32[]{:T(128)S(6)} %select_n.57), kind=kLoop, calls=%fused_computation.59 | loop fusion | bytes 8388612 | tf_op jit(solution)/shard_map/jit(dynamic_index_in_dim)/dynamic_slice | solution.py:68
  385.5 10.9 %copy.41 = f32[512,4,2,1,256]{0,4,2,1,3:T(8,128)} copy(f32[512,4,2,1,256]{4,3,2,1,0:T(1,128)} %constant_dynamic-slice_fusion.2) | data formatting | bytes 8388608 | tf_op jit(solution)/shard_map/jit(dynamic_index_in_dim)/dynamic_slice | solution.py:68
  396.4 17.5 %convolution_multiply_fusion = f32[2048,1024]{1,0:T(8,128)} fusion(f32[512,2048]{0,1:T(8,128)} %bitcast.107, f32[256,1024]{1,0:T(8,128)S(1)} %slice.92, f32[256,1024]{1,0:T(8,128)S(1)} %slice.86), kind=kOutput, calls=%fused_computation.5 | convolution fusion | flops 12887523328 | bytes 14680064 | tf_op jit(solution)/shard_map/dot_general | solution.py:70
  413.9 13.5 %reshape.102 = f32[8,1,256,4,1,256]{5,4,3,2,1,0:T(1,128)} reshape(f32[2048,1024]{1,0:T(8,128)} %convolution_multiply_fusion) | data formatting | bytes 16777216 | tf_op jit(solution)/shard_map/reshape | solution.py:73
  (48 shorter events, 22.2 us)
Async XLA Ops:
  7.2 85.8 %all-gather.8.cloned.1.call-start = ((), (), s32[]{:S(2)}) async-start(), calls=%async_computation.2 | async-start | bytes 9437184 | tf_op jit(solution)/shard_map/all_gather | solution.py:12
  39.2 109.9 %all-gather.10.cloned.1.call-start = ((), (), s32[]{:S(2)}) async-start(), calls=%async_computation.3 | async-start | bytes 9437184 | tf_op jit(solution)/shard_map/all_gather | solution.py:12
  98.8 251.8 %all-gather.6.cloned.1.call-start = ((), (), s32[]{:S(2)}) async-start(), calls=%async_computation.1 | async-start | bytes 35651584 | tf_op jit(solution)/shard_map/all_gather | solution.py:64
  193.6 16.6 %copy-start = (f32[8,256,1024]{1,2,0:T(8,128)S(1)}, f32[8,256,1024]{1,2,0:T(8,128)}, u32[]{:S(2)}) copy-start(f32[8,256,1024]{1,2,0:T(8,128)} %convolution_bitcast_fusion.1) | copy-start | bytes 25165828
  193.6 16.6 %copy-start.1 = (f32[256,1024]{0,1:T(8,128)S(1)}, f32[256,1024]{0,1:T(8,128)}, u32[]{:S(2)}) copy-start(f32[256,1024]{0,1:T(8,128)} %copy.48) | copy-start | bytes 3145732
  220.9 53.6 %all-to-all-start = ((f32[4,1,256,1,8,128]{5,2,0,3,1,4:T(8,128)}), f32[4,1,256,1,8,128]{5,2,0,3,1,4:T(8,128)}, u32[]{:S(2)}, u32[]{:S(2)}) async-start(f32[4,1,256,1,8,128]{5,2,0,3,1,4:T(8,128)} %copy.49), calls=%async_computation | async-start | bytes 8388608 | tf_op jit(solution)/shard_map/all_to_all | solution.py:76
Sparse Core Ops, SparseCore 0:
  39.3 53.6 all-gather.7
  98.9 50.1 all-gather.9
  154.0 196.5 all-gather.5
where the time goes:
time: 441 us; the launch traced here: 434 us
  waiting for transfers between devices  188 us (43%)
  local copies, waits for them, and re-layouts  117 us (27%)
  matrix products  57.8 us (13%)
  other arithmetic  50.2 us (11%)
  between operations  15.5 us (4%)
  starting transfers between devices  5.49 us (1%)
    all_gather x2, waiting for transfers between devices, picked(): lax.all_gather(value, axis)  74.1 us
    all_gather x1, waiting for transfers between devices, per_device(): lax.all_gather(stacked.reshape(depth, blocks_cols, 1, width), 'col', axis...  64.7 us
    all_to_all x1, waiting for transfers between devices, per_device(): lax.all_to_all(finished, 'row', split_axis=4, concat_axis=1, tiled=True)  48.9 us
    another operation x6, other arithmetic, solve_row(): lax.linalg.triangular_solve(diagonal, slab, left_side=True, lower=True)  42.5 us
    dot_general x3, matrix products, eliminate(): jnp.einsum('rab,bc->rac', column_part, solved, precision=lax.Precision.HI...  36.6 us
    unnamed x7, local copies, waits for them, and re-layouts  32.5 us
    all_gather x1, local copies, waits for them, and re-layouts, per_device(): lax.all_gather(stacked.reshape(depth, blocks_cols, 1, width), 'col', axis...  28.3 us
    dynamic_slice x2, local copies, waits for them, and re-layouts, per_device(): chosen = lax.dynamic_index_in_dim(gathered, row_index, 3, keepdims=False)  17.6 us
  transfers between devices with their start and end apart: 4, of which 4 were waited for; matrix products, arithmetic and copies ran while one was open for 24% of the time, Pallas kernels for 0%

commit v1 on v0

--- a/solution.py
+++ b/solution.py
@@ -1,3 +1,4 @@
+import functools
 import jax
 import jax.numpy as jnp
 from jax import lax
@@ -6,6 +7,15 @@
 BLK = 256
 K = 30
 STEPS = 2
+
+
+def name_the_bench(xx, net_axis):
+    s_next = jnp.stack([xx for _ in range(jax.lax.axis_size(net_axis))], axis=0)
+    newest = jax.lax.all_to_all(s_next, net_axis, 0, 0)
+    return jnp.concatenate(newest, axis=2)
+
+
+_unite_frames = functools.partial(name_the_bench, net_axis="col")
 
 
 def picked(value, axis, root):
@@ -61,9 +71,7 @@
     stacked = jnp.concatenate(solved_list, 0)
     depth = stacked.shape[0]
     owners_count = col_count // row_count
-    gathered = lax.all_gather(
-        stacked.reshape(depth, blocks_cols, 1, width), "col", axis=2, tiled=True
-    )
+    gathered = _unite_frames(stacked.reshape(depth, blocks_cols, 1, width))
     gathered = gathered.reshape(depth, blocks_cols, owners_count, row_count, width)
     chosen = lax.dynamic_index_in_dim(gathered, row_index, 3, keepdims=False)
     row_panels = chosen.reshape(depth, blocks_rows * width)

time: 441 us -> 843 us (1.91)
  waiting for transfers between devices: 188 us -> 570 us
  local copies, waits for them, and re-layouts: 117 us -> 128 us
    all_to_all x0 -> x1, waiting for transfers between devices: none -> 489 us  [name_the_bench(): newest = jax.lax.all_to_all(s_next, net_axis, 0, 0)]
    all_gather x1 -> x0, waiting for transfers between devices: 64.7 us -> none  [per_device(): lax.all_gather(stacked.reshape(depth, blocks_cols, 1, width), 'col', axis...]
    all_gather x2, waiting for transfers between devices: 74.1 us -> 37.8 us  [picked(): lax.all_gather(value, axis)]
    all_gather x1 -> x0, local copies, waits for them, and re-layouts: 28.3 us -> none  [per_device(): lax.all_gather(stacked.reshape(depth, blocks_cols, 1, width), 'col', axis...]
    all_to_all x0 -> x1, local copies, waits for them, and re-layouts: none -> 28.2 us  [name_the_bench(): newest = jax.lax.all_to_all(s_next, net_axis, 0, 0)]
    another operation x0 -> x1, local copies, waits for them, and re-layouts: none -> 12.3 us  [name_the_bench(): s_next = jnp.stack([xx for _ in range(jax.lax.axis_size(net_axis))], axis=0)]
    unnamed x7 -> x5, local copies, waits for them, and re-layouts: 32.5 us -> 32.2 us
  transfers between devices with their start and end apart: 4 -> 4, of which waited for: 4 -> 4; matrix products, arithmetic and copies ran while one was open for 24% -> 10% of each run, Pallas kernels for 0% -> 0%
where the time goes in v1:
time: 843 us; the launch traced here: 835 us
  waiting for transfers between devices  570 us (68%)
  local copies, waits for them, and re-layouts  128 us (15%)
  matrix products  57.9 us (7%)
  other arithmetic  50.9 us (6%)
  between operations  15.7 us (2%)
  starting transfers between devices  11.9 us (1%)
    all_to_all x1, waiting for transfers between devices, name_the_bench(): newest = jax.lax.all_to_all(s_next, net_axis, 0, 0)  489 us
    all_to_all x1, waiting for transfers between devices, per_device(): lax.all_to_all(finished, 'row', split_axis=4, concat_axis=1, tiled=True)  44 us
    another operation x6, other arithmetic, solve_row(): lax.linalg.triangular_solve(diagonal, slab, left_side=True, lower=True)  42.5 us
    all_gather x2, waiting for transfers between devices, picked(): lax.all_gather(value, axis)  37.8 us
    dot_general x3, matrix products, eliminate(): jnp.einsum('rab,bc->rac', column_part, solved, precision=lax.Precision.HI...  36.7 us
    unnamed x5, local copies, waits for them, and re-layouts  32.2 us
    all_to_all x1, local copies, waits for them, and re-layouts, name_the_bench(): newest = jax.lax.all_to_all(s_next, net_axis, 0, 0)  28.2 us
    dynamic_slice x2, local copies, waits for them, and re-layouts, per_device(): chosen = lax.dynamic_index_in_dim(gathered, row_index, 3, keepdims=False)  17.6 us
  transfers between devices with their start and end apart: 4, of which 4 were waited for; matrix products, arithmetic and copies ran while one was open for 10% of the time, Pallas kernels for 0%

profile of v1, /device:TPU:1, one launch (start us, length us, event | category | flops | bytes accessed | tf_op | source)
XLA Modules:
  0.0 835.2 jit_solution(3478437176535402484)
XLA Ops:
  8.4 4.0 while.4
  12.4 19.7 %custom-call.4 = f32[2,128,128]{1,2,0:T(8,128)S(1)} custom-call(f32[2,128,128]{2,1,0:T(8,128)S(1)} %get-tuple-element.17), custom_call_target="InvertDiagBlocksLowerTriangular" | custom-call | tf_op jit(solution)/shard_map/triangular_solve/custom-call.1 | solution.py:40
  32.0 4.2 slice_reduce_fusion
  42.4 3.8 while.5
  46.2 19.7 %custom-call.5 = f32[2,128,128]{1,2,0:T(8,128)S(1)} custom-call(f32[2,128,128]{2,1,0:T(8,128)S(1)} %get-tuple-element.18), custom_call_target="InvertDiagBlocksLowerTriangular" | custom-call | tf_op jit(solution)/shard_map/triangular_solve/custom-call.1 | solution.py:40
  65.9 27.3 %all-gather.5.cloned.1.call-done = f32[2048,1024]{1,0:T(8,128)} async-done(((f32[256,1024]{1,0:T(8,128)}), f32[2048,1024]{1,0:T(8,128)}) %all-gather.5.cloned.1.call-update) | async-done | bytes 8388624 | tf_op jit(solution)/shard_map/all_gather | solution.py:22
  99.0 20.8 %copy.38 = f32[8,1,256,4,1,256]{2,5,3,0,4,1:T(8,128)} copy(f32[8,1,256,4,1,256]{5,4,3,2,1,0:T(1,128)} %param.4) | data formatting | bytes 16777216 | tf_op args[0]
  121.5 17.4 %convolution_bitcast_fusion.1 = f32[8,256,1024]{1,2,0:T(8,128)} fusion(f32[2,8,1,256,256]{4,3,1,2,0:T(8,128)} %bitcast.114, f32[2048,1024]{1,0:T(8,128)} %all-gather.5.cloned.1.call-done), kind=kOutput, calls=%fused_computation.11 | convolution fusion | flops 6442450944 | bytes 11534336 | tf_op jit(solution)/shard_map/rab,bc->rac/dot_general | solution.py:45
  138.8 10.5 %all-gather.7.cloned.1.call-done = f32[2048,1024]{1,0:T(8,128)} async-done(((f32[256,1024]{1,0:T(8,128)}), f32[2048,1024]{1,0:T(8,128)}) %all-gather.7.cloned.1.call-update) | async-done | bytes 8388624 | tf_op jit(solution)/shard_map/all_gather | solution.py:22
  152.0 16.5 %convolution_bitcast_fusion = f32[8,256,1024]{1,2,0:T(8,128)S(1)} fusion(f32[2,8,1,256,256]{4,3,1,2,0:T(8,128)} %bitcast.115, f32[2048,1024]{1,0:T(8,128)} %all-gather.7.cloned.1.call-done), kind=kOutput, calls=%fused_computation.10 | convolution fusion | flops 6442450944 | bytes 11534336 | tf_op jit(solution)/shard_map/rab,bc->rac/dot_general | solution.py:45
  168.5 5.4 fusion
  173.8 5.3 copy.45
  179.1 4.7 all-to-all-start.1
  185.8 3.0 maximum_bitcast_fusion
  188.8 44.0 %all-to-all-done.1 = f32[4,1,256,1,8,128]{5,2,0,3,1,4:T(8,128)} async-done(((f32[4,1,256,1,8,128]{5,2,0,3,1,4:T(8,128)}), f32[4,1,256,1,8,128]{5,2,0,3,1,4:T(8,128)}, u32[]{:S(2)}, u32[]{:S(2)}) %all-to-all-start.1) | async-done | bytes 4194336 | tf_op jit(solution)/shard_map/all_to_all | solution.py:84
  232.7 12.3 %stack.3 = f32[16,512,4,1,256]{4,2,1,3,0:T(4,128)} broadcast(f32[512,4,256]{2,1,0:T(4,128)} %maximum_bitcast_fusion), dimensions={1,2,4} | broadcast | bytes 35651584 | tf_op jit(solution)/shard_map/stack | solution.py:13
  245.1 6.6 all-to-all-start
  251.7 11.2 %copy.47 = f32[4,8,256,1,1,128]{5,4,3,2,1,0:T(1,128)} copy(f32[4,8,256,1,1,128]{5,2,0,1,4,3:T(8,128)} %bitcast.28) | data formatting | bytes 8388608
  262.9 488.5 %all-to-all-done = f32[16,512,4,1,256]{4,2,1,3,0:T(4,128)} async-done(((f32[16,512,4,1,256]{4,2,1,3,0:T(4,128)}), f32[16,512,4,1,256]{4,2,1,3,0:T(4,128)}, u32[]{:S(2)}, u32[]{:S(2)}) %all-to-all-start) | async-done | bytes 33554464 | tf_op jit(solution)/shard_map/all_to_all | solution.py:14
  751.4 28.2 %copy.55 = f32[16,512,4,1,256]{4,0,2,1,3:T(8,128)S(1)} copy(f32[16,512,4,1,256]{4,2,1,3,0:T(4,128)} %all-to-all-done) | data formatting | bytes 67108864 | tf_op jit(solution)/shard_map/all_to_all | solution.py:14
  779.6 6.6 constant_dynamic-slice_fusion.2
  786.3 10.9 %copy.37 = f32[512,4,2,1,256]{0,4,2,1,3:T(8,128)} copy(f32[512,4,2,1,256]{4,3,2,1,0:T(1,128)} %constant_dynamic-slice_fusion.2) | data formatting | bytes 8388608 | tf_op jit(solution)/shard_map/jit(dynamic_index_in_dim)/dynamic_slice | solution.py:76
  797.2 17.5 %convolution_multiply_fusion = f32[2048,1024]{1,0:T(8,128)} fusion(f32[512,2048]{0,1:T(8,128)} %bitcast.111, f32[256,1024]{1,0:T(8,128)S(1)} %slice.92, f32[256,1024]{1,0:T(8,128)S(1)} %slice.86), kind=kOutput, calls=%fused_computation.5 | convolution fusion | flops 12887523328 | bytes 14680064 | tf_op jit(solution)/shard_map/dot_general | solution.py:78
  814.7 13.5 %reshape.104 = f32[8,1,256,4,1,256]{5,4,3,2,1,0:T(1,128)} reshape(f32[2048,1024]{1,0:T(8,128)} %convolution_multiply_fusion) | data formatting | bytes 16777216 | tf_op jit(solution)/shard_map/reshape | solution.py:81
  (44 shorter events, 25.7 us)
Async XLA Ops:
  7.2 86.0 %all-gather.5.cloned.1.call-start = ((), (), s32[]{:S(2)}) async-start(), calls=%async_computation.2 | async-start | bytes 9437184 | tf_op jit(solution)/shard_map/all_gather | solution.py:22
  39.3 110.0 %all-gather.7.cloned.1.call-start = ((), (), s32[]{:S(2)}) async-start(), calls=%async_computation.3 | async-start | bytes 9437184 | tf_op jit(solution)/shard_map/all_gather | solution.py:22
  152.0 16.5 %copy-start = (f32[256,1024]{0,1:T(8,128)S(1)}, f32[256,1024]{0,1:T(8,128)}, u32[]{:S(2)}) copy-start(f32[256,1024]{0,1:T(8,128)} %copy.44) | copy-start | bytes 3145732
  179.1 53.6 %all-to-all-start.1 = ((f32[4,1,256,1,8,128]{5,2,0,3,1,4:T(8,128)}), f32[4,1,256,1,8,128]{5,2,0,3,1,4:T(8,128)}, u32[]{:S(2)}, u32[]{:S(2)}) async-start(f32[4,1,256,1,8,128]{5,2,0,3,1,4:T(8,128)} %copy.45), calls=%async_computation.1 | async-start | bytes 8388608 | tf_op jit(solution)/shard_map/all_to_all | solution.py:84
  245.1 506.3 %all-to-all-start = ((f32[16,512,4,1,256]{4,2,1,3,0:T(4,128)}), f32[16,512,4,1,256]{4,2,1,3,0:T(4,128)}, u32[]{:S(2)}, u32[]{:S(2)}) async-start(f32[16,512,4,1,256]{4,2,1,3,0:T(4,128)} %stack.3), calls=%async_computation | async-start | bytes 67108864 | tf_op jit(solution)/shard_map/all_to_all | solution.py:14
Sparse Core Ops, SparseCore 0:
  39.5 53.6 all-gather.4
  99.1 50.1 all-gather.6
